TPU v7x, 32 devices: a whole 2x2x4 slice. The times are simulated.
32 devices in a mesh: parts: 2 (over x), owner: 16 (over z, y, core).
Axes of the slice: x: 2, y: 2, z: 4, core: 2. Of those that a mesh axis runs over, the one named last changes fastest.
Arguments:
- embeddings: bfloat16 [131072, 768], P(('parts', 'owner')), parts along dimension 0, may hold values from -6 to 6
- cluster_ids: int32 [131072], P(('parts', 'owner')), parts along dimension 0, may hold values from 0 to 63, as said below
- member_ranks: int32 [131072], P(('parts', 'owner')), parts along dimension 0, may hold values from 0 to 2047, as said below
Outputs:
- max_similarity: float32 [131072], P(('parts', 'owner')), parts along dimension 0
There are 2 independent parts, one for each index of `parts`. A program takes and returns all parts, laid end to end along the dimension named above; each array names one. Nothing has to cross between parts.
Inputs may be any that keep to these rules, and one draw needn't show every extreme that they name: `cluster_ids`: A cluster holds at most 2048 rows, and some cluster holds exactly 2048. At most 128 rows of one device belong to one cluster, reached on every device. For every o, the rows of one device with ids from 4 * o to 4 * o + 3 number at most 512, reached on every device. For every k, the rows of one device with ids from 2 * 4 * k to 2 * 4 * k + 2 * 4 - 1 number at most 512, reached on every device. `member_ranks`: within each cluster of s rows the ranks of its rows are 0 to s - 1, each once.
All inputs are finite; a program needn't handle non-finite values.
Results may differ from a plain program's by a relative error of at most 0.0003.
Values may be sent and summed in bfloat16 or wider, within the bound.
No kernel may reach another device: no remote copies, remote signals or barrier semaphores. Data moves between devices by JAX's collectives and lax.ppermute only.
A program may use at most 128 MiB of HBM per device.

v0:
```python
import jax
import jax.numpy as jnp
from jax import lax
from jax.sharding import PartitionSpec as P

CL_DEV = 4
BLK = 128
CMAX = 2048


epsilon = 1e-06
per_turn = 4


def order_within(destination, bins):
    onehot = (destination[:, None] == jnp.arange(bins, dtype=jnp.int32)[None, :]).astype(jnp.int32)
    return (jnp.sum(onehot * (jnp.cumsum(onehot, 0) - 1), 1), jnp.sum(onehot, 0), onehot)


def pack_send(embeddings, destination, order_in, slot_here, member_ranks, owners, slot_room):
    width = embeddings.shape[1]
    target = destination * slot_room + order_in
    send_rows = jnp.zeros((owners * slot_room, width), embeddings.dtype).at[target].set(embeddings)
    send_slot = jnp.full((owners * slot_room,), -1, jnp.int32).at[target].set(slot_here)
    send_rank = jnp.full((owners * slot_room,), -1, jnp.int32).at[target].set(member_ranks)
    meta_info = jnp.stack(
        [send_slot.reshape(owners, slot_room), send_rank.reshape(owners, slot_room)], 1
    )
    return (send_rows.reshape(owners, slot_room, width), meta_info, target)


def cluster_max(query_rows, query_slot, query_rank, column_rows, column_slot, column_rank, slots):
    width = query_rows.shape[1]
    block_room = per_turn * BLK
    slot_list = jnp.arange(slots, dtype=jnp.int32)
    column_match = column_slot[:, None] == slot_list[None, :]
    column_count = jnp.sum(column_match.astype(jnp.int32), 0)
    column_round = (column_count + BLK - 1) // BLK * BLK
    column_offset = jnp.cumsum(column_round) - column_round
    column_len = column_rows.shape[0] + slots * BLK + CMAX
    column_where = jnp.where(
        column_slot >= 0,
        jnp.sum(jnp.where(column_match, column_offset[None, :], 0), 1) + column_rank,
        column_len,
    )
    column_pack = (
        jnp.zeros((column_len, width), query_rows.dtype)
        .at[column_where]
        .set(column_rows, mode="drop")
    )
    column_inv = lax.rsqrt(jnp.sum(jnp.square(column_pack.astype(jnp.float32)), 1) + epsilon)
    query_order, query_count, query_match = order_within(query_slot, slots)
    query_turns = (query_count + block_room - 1) // block_room
    query_offset = (jnp.cumsum(query_turns) - query_turns) * block_room
    query_len = query_rows.shape[0] + slots * block_room
    query_where = jnp.where(
        query_slot >= 0, jnp.sum(query_match * query_offset[None, :], 1) + query_order, query_len
    )
    query_pack = (
        jnp.zeros((query_len, width), query_rows.dtype).at[query_where].set(query_rows, mode="drop")
    )
    query_ranks = jnp.zeros((query_len,), jnp.int32).at[query_where].set(query_rank, mode="drop")
    query_inv = lax.rsqrt(jnp.sum(jnp.square(query_pack.astype(jnp.float32)), 1) + epsilon)
    column_list = jnp.arange(CMAX, dtype=jnp.int32)
    best_sim = jnp.zeros((query_len,), jnp.float32)
    for slot in range(slots):
        column_block = lax.dynamic_slice_in_dim(column_pack, column_offset[slot], CMAX, 0)
        column_scale = lax.dynamic_slice_in_dim(column_inv, column_offset[slot], CMAX, 0)
        slot_start = query_offset[slot]

        def one_turn(turn_index, best_now):
            row_start = slot_start + turn_index * block_room
            row_block = lax.dynamic_slice_in_dim(query_pack, row_start, block_room, 0)
            row_inv = lax.dynamic_slice_in_dim(query_inv, row_start, block_room, 0)
            row_rank = lax.dynamic_slice_in_dim(query_ranks, row_start, block_room, 0)
            scores = lax.dot_general(
                row_block,
                column_block,
                (((1,), (1,)), ((), ())),
                preferred_element_type=jnp.float32,
            )
            scores = scores * row_inv[:, None] * column_scale[None, :]
            earlier = column_list[None, :] < row_rank[:, None]
            top_sim = jnp.max(jnp.where(earlier, scores, -1.0), 1)
            return lax.dynamic_update_slice(best_now, top_sim, (row_start,))

        best_sim = lax.fori_loop(0, query_turns[slot], one_turn, best_sim)
    return best_sim[jnp.minimum(query_where, query_len - 1)]


def on_device(embeddings, cluster_ids, member_ranks):
    row_count, width = embeddings.shape
    owners = lax.axis_size("owner")
    capacity = 2 * row_count // owners
    destination = cluster_ids // CL_DEV
    slot_here = cluster_ids % CL_DEV
    order_in, dest_sizes, dest_hot = order_within(destination, owners)
    send_rows, meta_info, target = pack_send(
        embeddings, destination, order_in, slot_here, member_ranks, owners, capacity
    )
    got_rows, got_meta = (
        lax.all_to_all(send_rows, "owner", split_axis=0, concat_axis=0, tiled=True),
        lax.all_to_all(meta_info, "owner", split_axis=0, concat_axis=0, tiled=True),
    )
    got_rows = got_rows.reshape(owners * capacity, width)
    got_slot = got_meta[:, 0, :].reshape(-1)
    got_rank = got_meta[:, 1, :].reshape(-1)
    best_sim = cluster_max(got_rows, got_slot, got_rank, got_rows, got_slot, got_rank, CL_DEV)
    answer = jnp.where(got_slot >= 0, best_sim, 0.0).reshape(owners, capacity)
    returned = lax.all_to_all(answer, "owner", split_axis=0, concat_axis=0, tiled=True).reshape(-1)
    return returned[target]


def solution(mesh):
    in_specs = (P(("parts", "owner"), None), P(("parts", "owner")), P(("parts", "owner")))
    out_specs = P(("parts", "owner"))
    return jax.shard_map(
        on_device, mesh=mesh, in_specs=in_specs, out_specs=out_specs, check_vma=False
    )
```

profile of v0, /device:TPU:0, one launch (start us, length us, event | category | flops | bytes accessed | tf_op | source)
XLA Modules:
  0.0 656.1 jit_solution(6517428207890959130)
XLA Ops:
  0.0 0.7 add_select_fusion
  0.8 4.6 reduce-window.26
  5.4 0.5 slice_reduce_fusion
  5.9 0.2 reduce-window.29
  6.0 0.1 add_add_fusion
  6.2 0.2 fusion.23
  6.4 0.6 broadcast_clamp_fusion.1
  7.0 15.5 %scatter_custom_fusion = s32[8192]{0:T(1024)S(1)} fusion(s32[4096]{0:T(1024)S(1)} %get-tuple-element.381, s32[4096]{0:T(1024)S(1)} %get-tuple-element.397, s32[]{:T(128)} %constant.137.clone.1), kind=kCustom, calls=%fused_computation.76 | custom fusion | bytes 32772 | tf_op jit(solution)/shard_map/scatter | solution.py:24
  22.5 15.7 %scatter_custom_fusion.1 = s32[8192]{0:T(1024)S(1)} fusion(s32[4096]{0:T(1024)S(1)} %get-tuple-element.381, s32[4096]{0:T(1024)} %param.13, s32[]{:T(128)} %constant.137.clone.1), kind=kCustom, calls=%fused_computation.74 | custom fusion | bytes 33280 | tf_op jit(solution)/shard_map/scatter | solution.py:25
  38.3 0.7 pad_add_fusion
  38.9 7.4 %all-to-all-start = ((s32[16,2,512]{2,1,0:T(2,128)}), s32[16,2,512]{2,1,0:T(2,128)S(1)}, u32[]{:S(2)}, u32[]{:S(2)}) async-start(s32[16,2,512]{2,1,0:T(2,128)} %pad_add_fusion), calls=%async_computation | async-start | bytes 131072 | tf_op jit(solution)/shard_map/all_to_all | solution.py:103
  46.3 26.1 %scatter_custom_fusion.3 = bf16[8192,768]{1,0:T(8,128)(2,1)} fusion(s32[4096]{0:T(1024)S(1)} %get-tuple-element.381, bf16[4096,768]{1,0:T(8,128)(2,1)} %param.11, bf16[]{:T(256)} %constant.148.clone.1), kind=kCustom, calls=%fused_computation.34 | custom fusion | bytes 12583424 | tf_op jit(solution)/shard_map/scatter | solution.py:23
  72.5 6.3 all-to-all-start.1
  78.8 0.2 convert_reduce_fusion
  79.0 0.2 reduce-window.36
  79.2 0.2 reduce-window.39
  79.4 0.7 fusion.40
  85.1 1.2 reduce-window.37
  86.3 0.2 slice_reduce_fusion.1
  86.5 0.2 reduce-window.38
  86.8 0.1 add_bitcast_fusion
  86.9 0.3 select_reduce_fusion.4
  89.8 0.2 compare_select_fusion
  89.9 30.5 %scatter_custom_fusion.2 = s32[10240]{0:T(1024)S(1)} fusion(s32[8192]{0:T(1024)S(1)} %bitcast.112, s32[8192]{0:T(1024)S(1)} %bitcast.105, s32[]{:T(128)} %constant.139.clone.1), kind=kCustom, calls=%fused_computation.67 | custom fusion | bytes 40964 | tf_op jit(solution)/shard_map/scatter | solution.py:62
  120.4 0.6 fusion.42
  121.0 181.4 %all-to-all-done.1 = bf16[16,512,768]{2,1,0:T(8,128)(2,1)} async-done(((bf16[16,512,768]{2,1,0:T(8,128)(2,1)}), bf16[16,512,768]{2,1,0:T(8,128)(2,1)}, u32[]{:S(2)}, u32[]{:S(2)}) %all-to-all-start.1) | async-done | bytes 12582944 | tf_op jit(solution)/shard_map/all_to_all | solution.py:102
  302.5 45.7 %scatter_custom_fusion.4 = bf16[10240,768]{1,0:T(8,128)(2,1)} fusion(s32[8192]{0:T(1024)S(1)} %bitcast.113, bf16[8192,768]{1,0:T(8,128)(2,1)} %bitcast.16, bf16[]{:T(256)} %constant.148.clone.1), kind=kCustom, calls=%fused_computation.32 | custom fusion | bytes 15729152 | tf_op jit(solution)/shard_map/scatter | solution.py:60
  348.2 45.8 %scatter_custom_fusion.5 = bf16[10752,768]{1,0:T(8,128)(2,1)} fusion(s32[8192]{0:T(1024)S(1)} %bitcast.111, bf16[8192,768]{1,0:T(8,128)(2,1)} %bitcast.16, bf16[]{:T(256)} %constant.148.clone.1), kind=kCustom, calls=%fused_computation.30 | custom fusion | bytes 16515584 | tf_op jit(solution)/shard_map/scatter | solution.py:49
  394.1 7.4 %multiply_reduce_fusion = f32[10752]{0:T(1024)S(1)} fusion(bf16[10752,768]{1,0:T(8,128)(2,1)} %scatter_custom_fusion.5), kind=kLoop, calls=%fused_computation.28 | loop fusion | flops 24761856 | bytes 16558080 | tf_op jit(solution)/shard_map/reduce_sum | solution.py:51
  401.5 3.1 copy-done
  404.6 4.9 constant_dynamic-slice_fusion
  409.4 0.1 fusion.39
  409.5 6.9 %multiply_reduce_fusion.1 = f32[10240]{0:T(1024)S(1)} fusion(bf16[10240,768]{1,0:T(8,128)(2,1)} %scatter_custom_fusion.4), kind=kLoop, calls=%fused_computation.29 | loop fusion | flops 23582720 | bytes 15769600 | tf_op jit(solution)/shard_map/reduce_sum | solution.py:63
  416.5 12.5 %while.44 = (s32[]{:T(128)}, f32[10240]{0:T(1024)S(1)}, s32[]{:T(128)}, s32[]{:T(128)}, s32[10240]{0:T(1024)S(1)}, /*index=5*/bf16[10240,768]{1,0:T(8,128)(2,1)}...) while((s32[]{:T(128)}, f32[10240]{0:T(1024)S(1)}, ...), condition=%wide.region_21.22_spmd.clone, body=%wide.region_19.21_spmd.clone.sunk | while | flops 1615855104 | bytes 3958983 | solution.py:87
  417.7 0.1 dynamic_slice.109
  417.9 4.3 select_reduce_fusion.10
  422.1 0.3 dynamic_update_slice.20
  423.7 0.1 dynamic_slice.109
  423.8 4.3 select_reduce_fusion.10
  428.1 0.3 dynamic_update_slice.20
  428.9 12.7 %while.45 = (s32[]{:T(128)}, f32[10240]{0:T(1024)S(1)}, s32[]{:T(128)}, s32[]{:T(128)}, s32[10240]{0:T(1024)S(1)}, /*index=5*/bf16[10240,768]{1,0:T(8,128)(2,1)}...) while((s32[]{:T(128)}, f32[10240]{0:T(1024)S(1)}, ...), condition=%wide.region_24.25_spmd.clone, body=%wide.region_22.24_spmd.clone.sunk | while | flops 1615855104 | bytes 3958983 | solution.py:87
  430.3 0.1 dynamic_slice.112
  430.4 4.3 select_reduce_fusion.11
  434.7 0.3 dynamic_update_slice.21
  436.3 0.1 dynamic_slice.112
  436.5 4.3 select_reduce_fusion.11
  440.7 0.3 dynamic_update_slice.21
  441.7 12.8 %while.46 = (s32[]{:T(128)}, f32[10240]{0:T(1024)S(1)}, s32[]{:T(128)}, s32[]{:T(128)}, s32[10240]{0:T(1024)S(1)}, /*index=5*/bf16[10240,768]{1,0:T(8,128)(2,1)}...) while((s32[]{:T(128)}, f32[10240]{0:T(1024)S(1)}, ...), condition=%wide.region_27.28_spmd.clone, body=%wide.region_25.27_spmd.clone.sunk | while | flops 1615855104 | bytes 3958983 | solution.py:87
  443.2 0.1 dynamic_slice.115
  443.3 4.3 select_reduce_fusion.12
  447.6 0.3 dynamic_update_slice.22
  449.1 0.1 dynamic_slice.115
  449.3 4.3 select_reduce_fusion.12
  453.6 0.3 dynamic_update_slice.22
  454.5 10.8 %while.47 = (s32[]{:T(128)}, f32[10240]{0:T(1024)S(1)}, s32[]{:T(128)}, s32[]{:T(128)}, s32[10240]{0:T(1024)S(1)}, /*index=5*/bf16[10240,768]{1,0:T(8,128)(2,1)}...) while((s32[]{:T(128)}, f32[10240]{0:T(1024)S(1)}, ...), condition=%wide.region_30.31_spmd.clone, body=%wide.region_28.30_spmd.clone.sunk | while | flops 1615855104 | bytes 3958983 | solution.py:87
  455.8 0.1 dynamic_slice.118
  456.0 3.3 select_reduce_fusion.13
  459.3 0.3 dynamic_update_slice.23
  460.9 0.1 dynamic_slice.118
  461.1 3.3 select_reduce_fusion.13
  464.3 0.3 dynamic_update_slice.23
  465.3 45.5 %gather_fusion = f32[8192]{0:T(1024)S(1)} fusion(f32[10240]{0:T(1024)S(1)} %get-tuple-element.220, s32[8192]{0:T(1024)S(1)} %broadcast_clamp_fusion), kind=kCustom, calls=%fused_computation | custom fusion | bytes 98304 | tf_op jit(solution)/shard_map/gather | solution.py:88
  510.9 104.5 %all_to_all.16 = f32[16,1,512]{2,1,0:T(1,128)S(1)} all-to-all(f32[16,1,512]{2,1,0:T(1,128)S(1)} %broadcast_select_fusion), channel_id=1, replica_groups=mesh['parts'=2,'owner'=16] {'owner'}, dimensions={0} | all-to-all | bytes 65536 | tf_op jit(solution)/shard_map/all_to_all | solution.py:110
  615.4 40.5 %gather_fusion.1 = f32[4096]{0:T(1024)} fusion(f32[8192]{0:T(1024)S(1)} %bitcast.94, s32[4096]{0:T(1024)S(1)} %copy-done.1), kind=kCustom, calls=%fused_computation.1 | custom fusion | bytes 49152 | tf_op jit(solution)/shard_map/gather | solution.py:111
  (24 shorter events, 0.9 us)
Async XLA Ops:
  38.9 33.5 %all-to-all-start = ((s32[16,2,512]{2,1,0:T(2,128)}), s32[16,2,512]{2,1,0:T(2,128)S(1)}, u32[]{:S(2)}, u32[]{:S(2)}) async-start(s32[16,2,512]{2,1,0:T(2,128)} %pad_add_fusion), calls=%async_computation | async-start | bytes 131072 | tf_op jit(solution)/shard_map/all_to_all | solution.py:103
  72.5 230.0 %all-to-all-start.1 = ((bf16[16,512,768]{2,1,0:T(8,128)(2,1)}), bf16[16,512,768]{2,1,0:T(8,128)(2,1)}, u32[]{:S(2)}, u32[]{:S(2)}) async-start(bf16[16,512,768]{2,1,0:T(8,128)(2,1)} %bitcast.95), calls=%async_computation.1 | async-start | bytes 25165824 | tf_op jit(solution)/shard_map/all_to_all | solution.py:102
  394.0 10.5 %copy-start = (bf16[10752,768]{1,0:T(8,128)(2,1)S(1)}, bf16[10752,768]{1,0:T(8,128)(2,1)}, u32[]{:S(2)}) copy-start(bf16[10752,768]{1,0:T(8,128)(2,1)} %scatter_custom_fusion.5) | copy-start | bytes 49545220
  465.3 150.1 %copy-start.1 = (s32[4096]{0:T(1024)S(1)}, s32[4096]{0:T(1024)}, u32[]{:S(2)}) copy-start(s32[4096]{0:T(1024)} %get-tuple-element.380) | copy-start | bytes 49156
where the time goes:
time: 666 us; the launch traced here: 656 us
  local copies, waits for them, and re-layouts  279 us (42%)
  waiting for transfers between devices  181 us (27%)
  blocking collectives  104 us (16%)
  matrix products  32.2 us (5%)
  other arithmetic  24.3 us (4%)
  starting transfers between devices  13.6 us (2%)
  loops' own time  13 us (2%)
  between operations  7.98 us (1%)
    all_to_all x1, waiting for transfers between devices, on_device(): lax.all_to_all(send_rows, 'owner', split_axis=0, concat_axis=0, tiled=True)  181 us
    all_to_all x1, blocking collectives, on_device(): lax.all_to_all(answer, 'owner', split_axis=0, concat_axis=0, tiled=True)  104 us
    scatter x1, local copies, waits for them, and re-layouts, cluster_max(): column_pack = jnp.zeros((column_len, width), query_rows.dtype).at[column_...  45.8 us
    scatter x1, local copies, waits for them, and re-layouts, cluster_max(): jnp.zeros((query_len, width), query_rows.dtype).at[query_where]  45.7 us
    gather x1, local copies, waits for them, and re-layouts, cluster_max(): return best_sim[jnp.minimum(query_where, query_len - 1)]  45.5 us
    gather x1, local copies, waits for them, and re-layouts, on_device(): return returned[target]  40.5 us
    dot_general x8, matrix products, one_turn(): lax.dot_general(row_block, column_block, (((1,), (1,)), ((), ())), prefer...  32.2 us
    scatter x1, local copies, waits for them, and re-layouts, cluster_max(): jnp.zeros((query_len,), jnp.int32).at[query_where]  30.5 us
  transfers between devices with their start and end apart: 2, of which 1 were waited for; matrix products, arithmetic and copies ran while one was open for 9% of the time, Pallas kernels for 0%

commit v1 on v0

v1 whole, which is shorter than its diff:
```python
import functools

import jax
import jax.numpy as jnp
from jax import lax
from jax.experimental import pallas as pl
from jax.experimental.pallas import tpu as pltpu
from jax.sharding import PartitionSpec as P

CL_DEV = 4
CMAX = 2048
EPSILON = 1e-06
MASKED = -30000.0
GROUP = 2 * CL_DEV
LANES = 128
VMEM_LIMIT = 48 * 1024 * 1024


def params():
    return pltpu.CompilerParams(vmem_limit_bytes=VMEM_LIMIT)


def nt_dot(a, b):
    return lax.dot_general(a, b, (((1,), (1,)), ((), ())), preferred_element_type=jnp.float32)


def one_hot(condition):
    return jnp.where(condition, 1.0, 0.0).astype(jnp.bfloat16)


def tile_lanes(x, times):
    return jnp.concatenate([x] * times, 1)


def order_kernel(block_rows, ids_ref, ranks_ref, pos_ref, keys_ref, local_ref):
    rows = ids_ref.shape[1]
    clusters = local_ref.shape[0]
    chunk = 256
    cluster_iota = lax.broadcasted_iota(jnp.int32, (clusters, chunk), 0)
    before = one_hot(
        lax.broadcasted_iota(jnp.int32, (chunk, chunk), 0)
        < lax.broadcasted_iota(jnp.int32, (chunk, chunk), 1)
    )
    ones = jnp.ones((chunk, LANES), jnp.bfloat16)
    count = jnp.zeros((clusters, LANES), jnp.float32)
    for start in range(0, rows, chunk):
        hot = one_hot(ids_ref[:, start : start + chunk] == cluster_iota)
        prefix = jnp.dot(hot, before, preferred_element_type=jnp.float32)
        local_ref[:, start : start + chunk] = prefix + tile_lanes(count, chunk // LANES)
        count += jnp.dot(hot, ones, preferred_element_type=jnp.float32)
    lower = one_hot(
        lax.broadcasted_iota(jnp.int32, (clusters, clusters), 1)
        < lax.broadcasted_iota(jnp.int32, (clusters, clusters), 0)
    )
    offset = jnp.dot(lower, count.astype(jnp.bfloat16), preferred_element_type=jnp.float32)
    offset = tile_lanes(offset, chunk // LANES)
    high_rows = rows // LANES
    table = jnp.zeros((2 * high_rows, LANES), jnp.float32)
    high_iota = lax.broadcasted_iota(jnp.int32, (high_rows, chunk), 0)
    low_iota = lax.broadcasted_iota(jnp.int32, (LANES, chunk), 0)
    for start in range(0, rows, chunk):
        ids = ids_ref[:, start : start + chunk]
        place = jnp.where(
            ids == cluster_iota, local_ref[:, start : start + chunk] + offset, 0.0
        )
        position = jnp.sum(place, 0, keepdims=True).astype(jnp.int32)
        pos_ref[:, start : start + chunk] = position
        key = (ids & (GROUP - 1)) * CMAX + ranks_ref[:, start : start + chunk]
        high_hot = (position >> 7) == high_iota
        key_high = (key >> 7).astype(jnp.float32)
        key_low = (key & 127).astype(jnp.float32)
        left = jnp.concatenate(
            [jnp.where(high_hot, key_high, 0.0), jnp.where(high_hot, key_low, 0.0)], 0
        ).astype(jnp.bfloat16)
        table += nt_dot(left, one_hot((position & 127) == low_iota))
    keys = (table[:high_rows] * 128.0 + table[high_rows:]).astype(jnp.int32)
    per_block = block_rows // LANES
    for group in range(rows // block_rows):
        piece = keys[group * per_block : (group + 1) * per_block]
        keys_ref[2 * group] = piece
        keys_ref[2 * group + 1] = piece


def order_rows(ids, ranks, chips, block_rows):
    rows = ids.shape[0]
    return pl.pallas_call(
        functools.partial(order_kernel, block_rows),
        out_shape=(
            jax.ShapeDtypeStruct((1, rows), jnp.int32),
            jax.ShapeDtypeStruct((2 * chips, block_rows // LANES, LANES), jnp.int32),
        ),
        scratch_shapes=[pltpu.VMEM((chips * GROUP, rows), jnp.float32)],
        compiler_params=params(),
        cost_estimate=pl.CostEstimate(flops=10**9, bytes_accessed=10**5, transcendentals=0),
        name="order_rows",
    )(ids.reshape(1, rows), ranks.reshape(1, rows))


def pick_kernel(group_ref, pos_ref, rows_ref, out_ref, total):
    step = pl.program_id(0)
    block_rows, depth = out_ref.shape[0], rows_ref.shape[0]
    target = lax.broadcasted_iota(jnp.int32, (block_rows, depth), 0) + group_ref[0] * block_rows
    part = jnp.dot(one_hot(pos_ref[...] == target), rows_ref[...], preferred_element_type=jnp.float32)

    @pl.when(step == 0)
    def _():
        total[...] = part

    @pl.when(step > 0)
    def _():
        total[...] += part

    @pl.when(step == pl.num_programs(0) - 1)
    def _():
        out_ref[...] = total[...].astype(out_ref.dtype)


def pick_block(group, position, embeddings, block_rows):
    rows, width = embeddings.shape
    depth = 1024
    return pl.pallas_call(
        pick_kernel,
        grid_spec=pltpu.PrefetchScalarGridSpec(
            num_scalar_prefetch=1,
            grid=(rows // depth,),
            in_specs=[
                pl.BlockSpec((1, depth), lambda i, g: (0, i)),
                pl.BlockSpec((depth, width), lambda i, g: (i, 0)),
            ],
            out_specs=pl.BlockSpec((block_rows, width), lambda i, g: (0, 0)),
            scratch_shapes=[pltpu.VMEM((block_rows, width), jnp.float32)],
        ),
        out_shape=jax.ShapeDtypeStruct((block_rows, width), embeddings.dtype),
        compiler_params=params(),
        cost_estimate=pl.CostEstimate(
            flops=2 * block_rows * rows * width, bytes_accessed=2 * rows * width, transcendentals=0
        ),
        name="pick_block",
    )(group, position, embeddings)


def inverse_kernel(rows_ref, out_ref):
    count = rows_ref.shape[0]
    for start in range(0, count, LANES):
        x = rows_ref[start : start + LANES].astype(jnp.float32)
        inverse = lax.rsqrt(jnp.sum(x * x, 1, keepdims=True) + EPSILON)
        spread = jnp.transpose(jnp.broadcast_to(inverse, (LANES, LANES)))
        out_ref[:, start : start + LANES] = spread[0:1]


def inverse_norms(embeddings):
    rows, width = embeddings.shape
    block = 512
    return pl.pallas_call(
        inverse_kernel,
        grid=(rows // block,),
        in_specs=[pl.BlockSpec((block, width), lambda i: (i, 0))],
        out_specs=pl.BlockSpec((1, block), lambda i: (0, i)),
        out_shape=jax.ShapeDtypeStruct((1, rows), jnp.float32),
        compiler_params=params(),
        cost_estimate=pl.CostEstimate(
            flops=4 * rows * width, bytes_accessed=2 * rows * width, transcendentals=0
        ),
        name="inverse_norms",
    )(embeddings)


def lane_keys(keys_ref, index):
    keys = keys_ref[index]
    return jnp.concatenate([keys[i : i + 1] for i in range(keys.shape[0])], 1)


def best_of(columns, column_inverse, column_key, queries, query_key):
    count = queries.shape[0]
    scores = nt_dot(columns, queries)
    scores = scores * tile_lanes(column_inverse, count // LANES)
    rank = query_key & (CMAX - 1)
    base = query_key - rank
    earlier = (tile_lanes(column_key, count // LANES) ^ base) < rank
    scores = jnp.where(earlier, scores, MASKED)
    return jnp.max(scores.reshape(scores.shape[0] // 8, 8, count), 0)


def step_kernel(old, slot_ref, keys_ref, own_ref, other_ref, *refs):
    if old:
        (rows_ref, inverse_ref, spread_ref, best_in, rows_out, inverse_out, spread_out, best_out,
         running) = refs
    else:
        rows_out, inverse_out, spread_out, best_out, running = refs
    block = own_ref.shape[0]
    step = pl.program_id(0)
    tile = 256
    own_key = lane_keys(keys_ref, slot_ref[old, 0])

    @pl.when(step == 0)
    def _():
        for side, ref in ((0, own_ref), (1, other_ref)):
            rows_out[0, side] = ref[...]
            keys = keys_ref[slot_ref[old, side]]
            for start in range(0, block, LANES):
                x = ref[start : start + LANES].astype(jnp.float32)
                inverse = lax.rsqrt(jnp.sum(x * x, 1, keepdims=True) + EPSILON)
                inverse_out[0, side, start : start + LANES] = jnp.broadcast_to(inverse, (LANES, LANES))
                piece = start // LANES
                spread_out[0, side, start : start + LANES] = jnp.transpose(
                    jnp.broadcast_to(keys[piece : piece + 1], (LANES, LANES))
                )
        running[...] = jnp.full(running.shape, MASKED, jnp.float32)

    if old:

        @pl.when(step < old)
        def _():
            old_key = lane_keys(keys_ref, slot_ref[step, 0])
            old_best = best_in[0]
            new_best = running[...]
            for side, ref in ((0, own_ref), (1, other_ref)):
                for start in range(0, block, tile):
                    cut = slice(start, start + tile)
                    old_best = jnp.maximum(
                        old_best,
                        best_of(ref[cut], inverse_out[0, side, cut], spread_out[0, side, cut],
                                rows_ref[0, 0], old_key),
                    )
                    new_best = jnp.maximum(
                        new_best,
                        best_of(rows_ref[0, side, cut], inverse_ref[0, side, cut],
                                spread_ref[0, side, cut], own_ref[...], own_key),
                    )
            best_out[0] = old_best
            running[...] = new_best

    @pl.when(step == old)
    def _():
        new_best = running[...]
        for side, ref in ((0, own_ref), (1, other_ref)):
            for start in range(0, block, tile):
                cut = slice(start, start + tile)
                new_best = jnp.maximum(
                    new_best,
                    best_of(ref[cut], inverse_out[0, side, cut], spread_out[0, side, cut],
                            own_ref[...], own_key),
                )
        best_out[0] = new_best


def match_step(old, chips, slots, keys, own, other, state):
    block, width = own.shape

    def whole(shape):
        return pl.BlockSpec(shape, lambda i, s: (0,) * len(shape))

    def old_block(shape):
        return pl.BlockSpec(
            (1,) + shape, lambda i, s: (jnp.minimum(i, old - 1),) + (0,) * len(shape)
        )

    def new_block(shape):
        return pl.BlockSpec((1,) + shape, lambda i, s: (old,) + (0,) * len(shape))

    in_specs = [whole(keys.shape), whole((block, width)), whole((block, width))]
    if old:
        in_specs += [
            old_block((2, block, width)),
            old_block((2, block, LANES)),
            old_block((2, block, LANES)),
            old_block((8, block)),
        ]
    pairs = 2 * (2 * old + 1) * block * block
    return pl.pallas_call(
        functools.partial(step_kernel, old),
        grid_spec=pltpu.PrefetchScalarGridSpec(
            num_scalar_prefetch=1,
            grid=(old + 1,),
            in_specs=in_specs,
            out_specs=(
                new_block((2, block, width)),
                new_block((2, block, LANES)),
                new_block((2, block, LANES)),
                pl.BlockSpec((1, 8, block), lambda i, s: (i, 0, 0)),
            ),
            scratch_shapes=[pltpu.VMEM((8, block), jnp.float32)],
        ),
        out_shape=(
            jax.ShapeDtypeStruct((chips, 2, block, width), own.dtype),
            jax.ShapeDtypeStruct((chips, 2, block, LANES), jnp.float32),
            jax.ShapeDtypeStruct((chips, 2, block, LANES), jnp.int32),
            jax.ShapeDtypeStruct((chips, 8, block), jnp.float32),
        ),
        input_output_aliases={4 + i: i for i in range(4)} if old else {},
        compiler_params=params(),
        cost_estimate=pl.CostEstimate(
            flops=2 * pairs * width, bytes_accessed=4 * (old + 1) * block * width, transcendentals=0
        ),
        name="match_step",
    )(slots, keys, own, other, *state)


def answer_kernel(chip_ref, block_rows, table_ref, pos_ref, inverse_ref, out_ref):
    rows = pos_ref.shape[1]
    chunk = 512
    table = table_ref[...]
    high = table.astype(jnp.bfloat16)
    rest = table - high.astype(jnp.float32)
    middle = rest.astype(jnp.bfloat16)
    low = (rest - middle.astype(jnp.float32)).astype(jnp.bfloat16)
    high_iota = lax.broadcasted_iota(jnp.int32, (rows // LANES, chunk), 0)
    low_iota = lax.broadcasted_iota(jnp.int32, (LANES, chunk), 0)
    for start in range(0, rows, chunk):
        position = pos_ref[:, start : start + chunk] ^ (chip_ref[0] * block_rows)
        hot = one_hot((position >> 7) == high_iota)
        values = sum(
            lax.dot_general(part, hot, (((0,), (0,)), ((), ())), preferred_element_type=jnp.float32)
            for part in (high, middle, low)
        )
        best = jnp.sum(
            jnp.where((position & 127) == low_iota, values, 0.0), 0, keepdims=True
        )
        out_ref[:, start : start + chunk] = jnp.maximum(
            best * inverse_ref[:, start : start + chunk], -1.0
        )


def answer_rows(chip, table, position, inverse, block_rows):
    rows = position.shape[1]

    def body(chip_ref, *refs):
        answer_kernel(chip_ref, block_rows, *refs)

    return pl.pallas_call(
        body,
        in_specs=[pl.BlockSpec(memory_space=pltpu.SMEM)] + [pl.BlockSpec(memory_space=pltpu.VMEM)] * 3,
        out_shape=jax.ShapeDtypeStruct((1, rows), jnp.float32),
        compiler_params=params(),
        name="answer_rows",
    )(chip, table, position, inverse)


def on_device(embeddings, cluster_ids, member_ranks):
    rows, width = embeddings.shape
    owners = lax.axis_size("owner")
    chips = owners // 2
    block = rows // chips
    me = lax.axis_index("owner").astype(jnp.int32)
    chip, core = me // 2, me % 2

    def across(x, d):
        return lax.ppermute(x, "owner", [(i, i ^ (2 * d)) for i in range(owners)])

    def swap(x):
        return lax.ppermute(x, "owner", [(i, i ^ 1) for i in range(owners)])

    position, send_keys = order_rows(cluster_ids, member_ranks, chips, block)

    def pick(d):
        return pick_block((chip ^ d).reshape(1), position, embeddings, block)

    near = list(range(1, chips // 2))
    far = list(range(chips // 2, chips))
    sends = [far[0]]
    visits = [0]
    for a, b in zip(near, far[1:]):
        sends += [a, b]
    for a, b in zip(near, far):
        visits += [a, b]
    visits.append(far[-1])
    own = {d: across(pick(d), d) for d in sends}
    own[0] = pick(0)
    keys = lax.all_to_all(send_keys, "owner", split_axis=0, concat_axis=0, tiled=True)
    inverse = inverse_norms(embeddings)
    slots = jnp.stack(
        [jnp.stack([2 * (chip ^ d) + core, 2 * (chip ^ d) + 1 - core]) for d in visits]
    )
    state = ()
    for turn, d in enumerate(visits):
        state = match_step(turn, chips, slots, keys, own[d], swap(own[d]), state)
    best = jnp.max(state[3], 1)
    spots = {d: best[turn : turn + 1] for turn, d in enumerate(visits)}
    table = jnp.concatenate([spots[d] for d in range(chips)], 0)
    bit = 1
    while bit < chips:
        split = table.reshape(chips // (2 * bit), 2, bit, block)
        got = across(split[:, 1], bit)
        table = jnp.stack([split[:, 0], got], 1).reshape(chips, block)
        bit *= 2
    table = table.reshape(rows // LANES, LANES)
    answer = answer_rows(chip.reshape(1), table, position, inverse, block)
    return answer.reshape(rows)


def solution(mesh):
    in_specs = (P(("parts", "owner"), None), P(("parts", "owner")), P(("parts", "owner")))
    out_specs = P(("parts", "owner"))
    return jax.shard_map(
        on_device, mesh=mesh, in_specs=in_specs, out_specs=out_specs, check_vma=False
    )
```

time: 666 us -> 286 us (0.43); the launches traced: 656 us -> 285 us
  local copies, waits for them, and re-layouts: 279 us -> 2.7 us
  Pallas kernels: 0 us -> 165 us
  blocking collectives: 104 us -> 0 us
  waiting for transfers between devices: 181 us -> 91.2 us
  matrix products: 32.2 us -> 0 us
  other arithmetic: 24.3 us -> 0.39 us
  loops' own time: 13 us -> 0 us
  starting transfers between devices: 13.6 us -> 25.9 us
  between operations: 7.98 us -> 0.17 us
    scatter x6 -> x0, local copies, waits for them, and re-layouts: 179 us -> none  [the longest x1 45.8 us: cluster_max(): column_pack = jnp.zeros((column_len, width), query_rows.dtype).at[column_...]
    pallas_call x0 -> x19, Pallas kernels: none -> 165 us  [the longest x8 98 us: match_step(): pl.pallas_call(functools.partial(step_kernel, old), grid_spec=pltpu.Prefe...]
    all_to_all x2 -> x1, waiting for transfers between devices: 181 us -> 60.2 us  [on_device(): lax.all_to_all(send_keys, 'owner', split_axis=0, concat_axis=0, tiled=True)]
    all_to_all x1 -> x0, blocking collectives: 104 us -> none  [on_device(): lax.all_to_all(answer, 'owner', split_axis=0, concat_axis=0, tiled=True)]
    gather x2 -> x0, local copies, waits for them, and re-layouts: 86.1 us -> none  [the longest x1 45.5 us: cluster_max(): return best_sim[jnp.minimum(query_where, query_len - 1)]]
    dot_general x8 -> x0, matrix products: 32.2 us -> none  [one_turn(): lax.dot_general(row_block, column_block, (((1,), (1,)), ((), ())), prefer...]
    ppermute x0 -> x18, waiting for transfers between devices: none -> 31.1 us  [the longest x10 31 us: across(): return lax.ppermute(x, 'owner', [(i, i ^ 2 * d) for i in range(owners)])]
    ppermute x0 -> x18, starting transfers between devices: none -> 19.5 us  [the longest x10 17.6 us: across(): return lax.ppermute(x, 'owner', [(i, i ^ 2 * d) for i in range(owners)])]
  transfers between devices with their start and end apart: 2 -> 19, of which waited for: 1 -> 5; matrix products, arithmetic and copies ran while one was open for 9% -> 0% of each run, Pallas kernels for 0% -> 47%
where the time goes in v1:
time: 286 us; the launch traced here: 285 us
  Pallas kernels  165 us (58%)
  waiting for transfers between devices  91.2 us (32%)
  starting transfers between devices  25.9 us (9%)
    pallas_call x8, Pallas kernels, match_step(): pl.pallas_call(functools.partial(step_kernel, old), grid_spec=pltpu.Prefe...  98 us
    all_to_all x1, waiting for transfers between devices, on_device(): lax.all_to_all(send_keys, 'owner', split_axis=0, concat_axis=0, tiled=True)  60.2 us
    pallas_call x8, Pallas kernels, pick_block(): pl.pallas_call(pick_kernel, grid_spec=pltpu.PrefetchScalarGridSpec(num_sc...  56.9 us
    ppermute x10, waiting for transfers between devices, across(): return lax.ppermute(x, 'owner', [(i, i ^ 2 * d) for i in range(owners)])  31 us
    ppermute x10, starting transfers between devices, across(): return lax.ppermute(x, 'owner', [(i, i ^ 2 * d) for i in range(owners)])  17.6 us
    all_to_all x1, starting transfers between devices, on_device(): lax.all_to_all(send_keys, 'owner', split_axis=0, concat_axis=0, tiled=True)  6.41 us
    pallas_call x1, Pallas kernels, inverse_norms(): pl.pallas_call(inverse_kernel, grid=(rows // block,), in_specs=[pl.BlockS...  6.08 us
  transfers between devices with their start and end apart: 19, of which 5 were waited for; matrix products, arithmetic and copies ran while one was open for 0% of the time, Pallas kernels for 47%

profile of v1, /device:TPU:0, one launch (start us, length us, event | category | flops | bytes accessed | tf_op | source)
XLA Modules:
  0.0 285.4 jit_solution(18198536787648009497)
XLA Ops:
  0.0 0.7 copy-done.2
  0.7 0.7 copy-done.3
  1.4 2.3 order_rows.1
  3.8 6.3 %pick_block.15.own_ref = bf16[512,768]{1,0:T(8,128)(2,1)S(1)} custom-call(s32[1]{0:T(128)} %bitcast.group_ref.chip_ref, s32[1,4096]{1,0:T(1,128)S(1)} %get-tuple-element.37.pos_ref.refs_1_, bf16[4096,768]{1,0:T(8,128)(2,1)} %rows_ref.17), custom_call_target="tpu_custom_call" | custom-call | flops 3221225472 | bytes 6291456 | tf_op jit(solution)/shard_map/pick_block/pallas_call | solution.py:121
  10.1 0.5 collective-permute-start.14
  10.6 7.2 %pick_block.14 = bf16[512,768]{1,0:T(8,128)(2,1)} custom-call(s32[1]{0:T(128)} %bitcast.33.group_ref, s32[1,4096]{1,0:T(1,128)S(1)} %get-tuple-element.37.pos_ref.refs_1_, bf16[4096,768]{1,0:T(8,128)(2,1)} %rows_ref.17), custom_call_target="tpu_custom_call" | custom-call | flops 3221225472 | bytes 6291456 | tf_op jit(solution)/shard_map/pick_block/pallas_call | solution.py:121
  17.9 2.7 collective-permute-start.12
  20.6 7.2 %pick_block.13 = bf16[512,768]{1,0:T(8,128)(2,1)} custom-call(s32[1]{0:T(128)} %bitcast.32.group_ref, s32[1,4096]{1,0:T(1,128)S(1)} %get-tuple-element.37.pos_ref.refs_1_, bf16[4096,768]{1,0:T(8,128)(2,1)} %rows_ref.17), custom_call_target="tpu_custom_call" | custom-call | flops 3221225472 | bytes 6291456 | tf_op jit(solution)/shard_map/pick_block/pallas_call | solution.py:121
  27.8 2.6 collective-permute-start.10
  30.4 7.2 %pick_block.12 = bf16[512,768]{1,0:T(8,128)(2,1)} custom-call(s32[1]{0:T(128)} %bitcast.31.group_ref, s32[1,4096]{1,0:T(1,128)S(1)} %get-tuple-element.37.pos_ref.refs_1_, bf16[4096,768]{1,0:T(8,128)(2,1)} %rows_ref.17), custom_call_target="tpu_custom_call" | custom-call | flops 3221225472 | bytes 6291456 | tf_op jit(solution)/shard_map/pick_block/pallas_call | solution.py:121
  37.6 1.6 collective-permute-start.8
  39.2 7.2 %pick_block.11 = bf16[512,768]{1,0:T(8,128)(2,1)} custom-call(s32[1]{0:T(128)} %bitcast.30.group_ref, s32[1,4096]{1,0:T(1,128)S(1)} %get-tuple-element.37.pos_ref.refs_1_, bf16[4096,768]{1,0:T(8,128)(2,1)} %rows_ref.17), custom_call_target="tpu_custom_call" | custom-call | flops 3221225472 | bytes 6291456 | tf_op jit(solution)/shard_map/pick_block/pallas_call | solution.py:121
  46.4 0.3 collective-permute-start.6
  46.7 7.2 %pick_block.10 = bf16[512,768]{1,0:T(8,128)(2,1)} custom-call(s32[1]{0:T(128)} %bitcast.29.group_ref, s32[1,4096]{1,0:T(1,128)S(1)} %get-tuple-element.37.pos_ref.refs_1_, bf16[4096,768]{1,0:T(8,128)(2,1)} %rows_ref.17), custom_call_target="tpu_custom_call" | custom-call | flops 3221225472 | bytes 6291456 | tf_op jit(solution)/shard_map/pick_block/pallas_call | solution.py:121
  53.9 0.0 collective-permute-done.12.own_ref
  53.9 0.0 collective-permute-start.13
  53.9 7.2 %pick_block.9 = bf16[512,768]{1,0:T(8,128)(2,1)} custom-call(s32[1]{0:T(128)} %bitcast.28.group_ref, s32[1,4096]{1,0:T(1,128)S(1)} %get-tuple-element.37.pos_ref.refs_1_, bf16[4096,768]{1,0:T(8,128)(2,1)} %rows_ref.17), custom_call_target="tpu_custom_call" | custom-call | flops 3221225472 | bytes 6291456 | tf_op jit(solution)/shard_map/pick_block/pallas_call | solution.py:121
  61.2 7.2 %pick_block.8 = bf16[512,768]{1,0:T(8,128)(2,1)} custom-call(s32[1]{0:T(128)} %bitcast.27.group_ref, s32[1,4096]{1,0:T(1,128)S(1)} %get-tuple-element.37.pos_ref.refs_1_, bf16[4096,768]{1,0:T(8,128)(2,1)} %rows_ref.17), custom_call_target="tpu_custom_call" | custom-call | flops 3221225472 | bytes 6291456 | tf_op jit(solution)/shard_map/pick_block/pallas_call | solution.py:121
  68.4 0.0 collective-permute-done.14.other_ref
  68.4 1.4 collective-permute-start.4
  69.8 0.0 collective-permute-done.10.own_ref
  69.8 3.6 %collective-permute-start.2 = (bf16[512,768]{1,0:T(8,128)(2,1)}, bf16[512,768]{1,0:T(8,128)(2,1)}, u32[]{:S(2)}, u32[]{:S(2)}) collective-permute-start(bf16[512,768]{1,0:T(8,128)(2,1)} %pick_block.9), channel_id=1, source_target_pairs={{0,12},{1,13},{2,14},{3,15},{4,8},{5,9},{6,10},{7,11},{8,4},{9,5},... | collective-permute-start | bytes 2359304 | tf_op jit(solution)/shard_map/ppermute | solution.py:348
  73.4 1.5 collective-permute-done.8.own_ref
  75.0 0.2 collective-permute-start
  75.1 24.5 %collective-permute-done.6.own_ref = bf16[512,768]{1,0:T(8,128)(2,1)} collective-permute-done((bf16[512,768]{1,0:T(8,128)(2,1)}, bf16[512,768]{1,0:T(8,128)(2,1)}, u32[]{:S(2)}, u32[]{:S(2)}) %collective-permute-start.6) | collective-permute-done | bytes 786464 | tf_op jit(solution)/shard_map/ppermute | solution.py:348
  99.7 0.0 collective-permute-start.11
  99.7 6.4 %all-to-all-start = ((s32[16,4,128]{2,1,0:T(4,128)}), s32[16,4,128]{2,1,0:T(4,128)S(1)}, u32[]{:S(2)}, u32[]{:S(2)}) async-start(s32[16,4,128]{2,1,0:T(4,128)} %get-tuple-element.36), calls=%async_computation | async-start | bytes 65536 | tf_op jit(solution)/shard_map/all_to_all | solution.py:369
  106.1 0.1 add_bitcast_fusion.6
  106.2 0.1 add_bitcast_fusion.4
  106.3 0.1 add_bitcast_fusion.2
  106.4 0.0 collective-permute-done.13.other_ref
  106.4 0.4 collective-permute-start.9
  106.7 0.1 add_bitcast_fusion
  106.8 60.2 %all-to-all-done.keys_ref = s32[16,4,128]{2,1,0:T(4,128)S(1)} async-done(((s32[16,4,128]{2,1,0:T(4,128)}), s32[16,4,128]{2,1,0:T(4,128)S(1)}, u32[]{:S(2)}, u32[]{:S(2)}) %all-to-all-start) | async-done | bytes 32800 | tf_op jit(solution)/shard_map/all_to_all | solution.py:369
  167.0 1.1 copy-done.1
  168.1 4.1 %match_step.8 = (bf16[8,2,512,768]{3,2,1,0:T(8,128)(2,1)}, f32[8,2,512,128]{3,2,1,0:T(8,128)S(1)}, s32[8,2,512,128]{3,2,1,0:T(8,128)}, f32[8,8,512]{2,1,0:T(8,128)S(1)}) custom-call(s32[8,2]{1,0:T(8,128)S(1)} %stack.151.slot_ref, s32[16,4,128]{2,1,0:T(4,128)S(1)} %all-to-all-done.keys_ref, bf16[512,768]{1,0:T(8,128)(2,1)S(1)} %copy-done.1, ...), custom_call_target="tpu_custom_call" | custom-call | flops 805306368 | bytes 1572864 | tf_op jit(solution)/shard_map/match_step/pallas_call | solution.py:270
  172.2 7.3 %match_step.9 = (bf16[8,2,512,768]{3,2,1,0:T(8,128)(2,1)}, f32[8,2,512,128]{3,2,1,0:T(8,128)S(1)}, s32[8,2,512,128]{3,2,1,0:T(8,128)}, f32[8,8,512]{2,1,0:T(8,128)S(1)}) custom-call(s32[8,2]{1,0:T(8,128)S(1)} %stack.151.slot_ref, s32[16,4,128]{2,1,0:T(4,128)S(1)} %all-to-all-done.keys_ref, ...), custom_call_target="tpu_custom_call", output_to_operand_aliasing={{0}: (4, {}), {1}: (5, {}), {2}: (6, {}), {3}: (7, {})} | custom-call | flops 2415919104 | bytes 3145728 | tf_op jit(solution)/shard_map/match_step/pallas_call | solution.py:270
  179.5 0.0 collective-permute-done.4.own_ref
  179.5 0.1 collective-permute-start.7
  179.6 0.0 collective-permute-done.2.own_ref
  179.6 0.4 collective-permute-start.5
  180.0 0.0 collective-permute-done.own_ref
  180.0 0.1 collective-permute-start.3
  180.2 0.0 collective-permute-done.11.other_ref
  180.2 0.4 collective-permute-start.1
  180.6 9.1 %match_step.10 = (bf16[8,2,512,768]{3,2,1,0:T(8,128)(2,1)}, f32[8,2,512,128]{3,2,1,0:T(8,128)S(1)}, s32[8,2,512,128]{3,2,1,0:T(8,128)}, f32[8,8,512]{2,1,0:T(8,128)S(1)}) custom-call(s32[8,2]{1,0:T(8,128)S(1)} %stack.151.slot_ref, s32[16,4,128]{2,1,0:T(4,128)S(1)} %all-to-all-done.keys_ref, ...), custom_call_target="tpu_custom_call", output_to_operand_aliasing={{0}: (4, {}), {1}: (5, {}), {2}: (6, {}), {3}: (7, {})} | custom-call | flops 4026531840 | bytes 4718592 | tf_op jit(solution)/shard_map/match_step/pallas_call | solution.py:270
  189.6 0.0 collective-permute-done.9.other_ref
  189.6 11.4 %match_step.11 = (bf16[8,2,512,768]{3,2,1,0:T(8,128)(2,1)}, f32[8,2,512,128]{3,2,1,0:T(8,128)S(1)}, s32[8,2,512,128]{3,2,1,0:T(8,128)}, f32[8,8,512]{2,1,0:T(8,128)S(1)}) custom-call(s32[8,2]{1,0:T(8,128)S(1)} %stack.151.slot_ref, s32[16,4,128]{2,1,0:T(4,128)S(1)} %all-to-all-done.keys_ref, ...), custom_call_target="tpu_custom_call", output_to_operand_aliasing={{0}: (4, {}), {1}: (5, {}), {2}: (6, {}), {3}: (7, {})} | custom-call | flops 5637144576 | bytes 6291456 | tf_op jit(solution)/shard_map/match_step/pallas_call | solution.py:270
  201.0 0.0 collective-permute-done.7.other_ref
  201.0 13.7 %match_step.12 = (bf16[8,2,512,768]{3,2,1,0:T(8,128)(2,1)}, f32[8,2,512,128]{3,2,1,0:T(8,128)S(1)}, s32[8,2,512,128]{3,2,1,0:T(8,128)}, f32[8,8,512]{2,1,0:T(8,128)S(1)}) custom-call(s32[8,2]{1,0:T(8,128)S(1)} %stack.151.slot_ref, s32[16,4,128]{2,1,0:T(4,128)S(1)} %all-to-all-done.keys_ref, ...), custom_call_target="tpu_custom_call", output_to_operand_aliasing={{0}: (4, {}), {1}: (5, {}), {2}: (6, {}), {3}: (7, {})} | custom-call | flops 7247757312 | bytes 7864320 | tf_op jit(solution)/shard_map/match_step/pallas_call | solution.py:270
  214.7 0.0 collective-permute-done.5.other_ref
  214.7 15.5 %match_step.13 = (bf16[8,2,512,768]{3,2,1,0:T(8,128)(2,1)}, f32[8,2,512,128]{3,2,1,0:T(8,128)S(1)}, s32[8,2,512,128]{3,2,1,0:T(8,128)}, f32[8,8,512]{2,1,0:T(8,128)S(1)}) custom-call(s32[8,2]{1,0:T(8,128)S(1)} %stack.151.slot_ref, s32[16,4,128]{2,1,0:T(4,128)S(1)} %all-to-all-done.keys_ref, ...), custom_call_target="tpu_custom_call", output_to_operand_aliasing={{0}: (4, {}), {1}: (5, {}), {2}: (6, {}), {3}: (7, {})} | custom-call | flops 8858370048 | bytes 9437184 | tf_op jit(solution)/shard_map/match_step/pallas_call | solution.py:270
  230.2 0.0 collective-permute-done.3.other_ref
  230.2 17.5 %match_step.14 = (bf16[8,2,512,768]{3,2,1,0:T(8,128)(2,1)}, f32[8,2,512,128]{3,2,1,0:T(8,128)S(1)}, s32[8,2,512,128]{3,2,1,0:T(8,128)}, f32[8,8,512]{2,1,0:T(8,128)S(1)}) custom-call(s32[8,2]{1,0:T(8,128)S(1)} %stack.151.slot_ref, s32[16,4,128]{2,1,0:T(4,128)S(1)} %all-to-all-done.keys_ref, ...), custom_call_target="tpu_custom_call", output_to_operand_aliasing={{0}: (4, {}), {1}: (5, {}), {2}: (6, {}), {3}: (7, {})} | custom-call | flops 10468982784 | bytes 11010048 | tf_op jit(solution)/shard_map/match_step/pallas_call | solution.py:270
  247.7 0.0 collective-permute-done.1.other_ref
  247.7 19.5 %match_step.15 = (bf16[8,2,512,768]{3,2,1,0:T(8,128)(2,1)}, f32[8,2,512,128]{3,2,1,0:T(8,128)S(1)}, s32[8,2,512,128]{3,2,1,0:T(8,128)}, f32[8,8,512]{2,1,0:T(8,128)S(1)}) custom-call(s32[8,2]{1,0:T(8,128)S(1)} %stack.151.slot_ref, s32[16,4,128]{2,1,0:T(4,128)S(1)} %all-to-all-done.keys_ref, ...), custom_call_target="tpu_custom_call", output_to_operand_aliasing={{0}: (4, {}), {1}: (5, {}), {2}: (6, {}), {3}: (7, {})} | custom-call | flops 12079595520 | bytes 12582912 | tf_op jit(solution)/shard_map/match_step/pallas_call | solution.py:270
  267.4 1.6 collective-permute-start.15
  268.9 2.1 collective-permute-done.15
  271.1 0.9 collective-permute-start.16
  272.0 2.8 collective-permute-done.16
  274.9 2.7 collective-permute-start.17
  277.6 6.1 %inverse_norms.1.refs_2_ = f32[1,4096]{1,0:T(1,128)S(1)} custom-call(bf16[4096,768]{1,0:T(8,128)(2,1)} %rows_ref.17), custom_call_target="tpu_custom_call" | custom-call | flops 12582912 | bytes 6291456 | tf_op jit(solution)/shard_map/inverse_norms/pallas_call | solution.py:154
  283.7 0.0 collective-permute-done.17
  283.7 1.6 answer_rows.1
  (17 shorter events, 0.2 us)
Async XLA Ops:
  0.0 0.7 copy-start.2
  0.7 0.7 copy-start.3
  10.1 7.7 %copy-start = (bf16[512,768]{1,0:T(8,128)(2,1)}, bf16[512,768]{1,0:T(8,128)(2,1)S(1)}, u32[]{:S(2)}) copy-start(bf16[512,768]{1,0:T(8,128)(2,1)S(1)} %pick_block.15.own_ref) | copy-start | bytes 2359300
  10.1 58.3 %collective-permute-start.14 = (bf16[512,768]{1,0:T(8,128)(2,1)S(1)}, bf16[512,768]{1,0:T(8,128)(2,1)}, u32[]{:S(2)}, u32[]{:S(2)}) collective-permute-start(bf16[512,768]{1,0:T(8,128)(2,1)S(1)} %pick_block.15.own_ref), channel_id=1, source_target_pairs={{0,1},{1,0},{2,3},{3,2},{4,5},{5,4},{6,7},{7,6},{8,9},{9,8},{10,11... | collective-permute-start | bytes 2359304 | tf_op jit(solution)/shard_map/ppermute | solution.py:351
  17.9 36.1 %collective-permute-start.12 = (bf16[512,768]{1,0:T(8,128)(2,1)}, bf16[512,768]{1,0:T(8,128)(2,1)S(1)}, u32[]{:S(2)}, u32[]{:S(2)}) collective-permute-start(bf16[512,768]{1,0:T(8,128)(2,1)} %pick_block.14), channel_id=1, source_target_pairs={{0,2},{1,3},{2,0},{3,1},{4,6},{5,7},{6,4},{7,5},{8,10},{9,11},{10,... | collective-permute-start | bytes 2359304 | tf_op jit(solution)/shard_map/ppermute | solution.py:348
  27.8 42.0 %collective-permute-start.10 = (bf16[512,768]{1,0:T(8,128)(2,1)}, bf16[512,768]{1,0:T(8,128)(2,1)S(1)}, u32[]{:S(2)}, u32[]{:S(2)}) collective-permute-start(bf16[512,768]{1,0:T(8,128)(2,1)} %pick_block.13), channel_id=1, source_target_pairs={{0,8},{1,9},{2,10},{3,11},{4,12},{5,13},{6,14},{7,15},{8,0},{9,1},... | collective-permute-start | bytes 2359304 | tf_op jit(solution)/shard_map/ppermute | solution.py:348
  37.6 37.3 %collective-permute-start.8 = (bf16[512,768]{1,0:T(8,128)(2,1)}, bf16[512,768]{1,0:T(8,128)(2,1)S(1)}, u32[]{:S(2)}, u32[]{:S(2)}) collective-permute-start(bf16[512,768]{1,0:T(8,128)(2,1)} %pick_block.12), channel_id=1, source_target_pairs={{0,4},{1,5},{2,6},{3,7},{4,0},{5,1},{6,2},{7,3},{8,12},{9,13},{10,... | collective-permute-start | bytes 2359304 | tf_op jit(solution)/shard_map/ppermute | solution.py:348
  46.4 53.2 %collective-permute-start.6 = (bf16[512,768]{1,0:T(8,128)(2,1)}, bf16[512,768]{1,0:T(8,128)(2,1)}, u32[]{:S(2)}, u32[]{:S(2)}) collective-permute-start(bf16[512,768]{1,0:T(8,128)(2,1)} %pick_block.11), channel_id=1, source_target_pairs={{0,10},{1,11},{2,8},{3,9},{4,14},{5,15},{6,12},{7,13},{8,2},{9,3},... | collective-permute-start | bytes 2359304 | tf_op jit(solution)/shard_map/ppermute | solution.py:348
  53.9 52.4 %collective-permute-start.13 = (bf16[512,768]{1,0:T(8,128)(2,1)S(1)}, bf16[512,768]{1,0:T(8,128)(2,1)}, u32[]{:S(2)}, u32[]{:S(2)}) collective-permute-start(bf16[512,768]{1,0:T(8,128)(2,1)S(1)} %collective-permute-done.12.own_ref), channel_id=1, source_target_pairs={{0,1},{1,0},{2,3},{3,2},{4,5},{5,4},{6,7},{7,6},{8,9},{9,8},{10,11... | collective-permute-start | bytes 2359304 | tf_op jit(solution)/shard_map/ppermute | solution.py:351
  68.4 111.1 %collective-permute-start.4 = (bf16[512,768]{1,0:T(8,128)(2,1)}, bf16[512,768]{1,0:T(8,128)(2,1)}, u32[]{:S(2)}, u32[]{:S(2)}) collective-permute-start(bf16[512,768]{1,0:T(8,128)(2,1)} %pick_block.10), channel_id=1, source_target_pairs={{0,6},{1,7},{2,4},{3,5},{4,2},{5,3},{6,0},{7,1},{8,14},{9,15},{10,... | collective-permute-start | bytes 2359304 | tf_op jit(solution)/shard_map/ppermute | solution.py:348
  69.8 109.8 %collective-permute-start.2 = (bf16[512,768]{1,0:T(8,128)(2,1)}, bf16[512,768]{1,0:T(8,128)(2,1)}, u32[]{:S(2)}, u32[]{:S(2)}) collective-permute-start(bf16[512,768]{1,0:T(8,128)(2,1)} %pick_block.9), channel_id=1, source_target_pairs={{0,12},{1,13},{2,14},{3,15},{4,8},{5,9},{6,10},{7,11},{8,4},{9,5},... | collective-permute-start | bytes 2359304 | tf_op jit(solution)/shard_map/ppermute | solution.py:348
  75.0 105.1 %collective-permute-start = (bf16[512,768]{1,0:T(8,128)(2,1)}, bf16[512,768]{1,0:T(8,128)(2,1)}, u32[]{:S(2)}, u32[]{:S(2)}) collective-permute-start(bf16[512,768]{1,0:T(8,128)(2,1)} %pick_block.8), channel_id=1, source_target_pairs={{0,14},{1,15},{2,12},{3,13},{4,10},{5,11},{6,8},{7,9},{8,6},{9,7},... | collective-permute-start | bytes 2359304 | tf_op jit(solution)/shard_map/ppermute | solution.py:348
  99.7 80.5 %collective-permute-start.11 = (bf16[512,768]{1,0:T(8,128)(2,1)S(1)}, bf16[512,768]{1,0:T(8,128)(2,1)S(1)}, u32[]{:S(2)}, u32[]{:S(2)}) collective-permute-start(bf16[512,768]{1,0:T(8,128)(2,1)S(1)} %collective-permute-done.10.own_ref), channel_id=1, source_target_pairs={{0,1},{1,0},{2,3},{3,2},{4,5},{5,4},{6,7},{7,6},{8,9},{9,8},{10,11... | collective-permute-start | bytes 2359304 | tf_op jit(solution)/shard_map/ppermute | solution.py:351
  99.7 67.3 %all-to-all-start = ((s32[16,4,128]{2,1,0:T(4,128)}), s32[16,4,128]{2,1,0:T(4,128)S(1)}, u32[]{:S(2)}, u32[]{:S(2)}) async-start(s32[16,4,128]{2,1,0:T(4,128)} %get-tuple-element.36), calls=%async_computation | async-start | bytes 65536 | tf_op jit(solution)/shard_map/all_to_all | solution.py:369
  106.4 83.3 %collective-permute-start.9 = (bf16[512,768]{1,0:T(8,128)(2,1)S(1)}, bf16[512,768]{1,0:T(8,128)(2,1)}, u32[]{:S(2)}, u32[]{:S(2)}) collective-permute-start(bf16[512,768]{1,0:T(8,128)(2,1)S(1)} %collective-permute-done.8.own_ref), channel_id=1, source_target_pairs={{0,1},{1,0},{2,3},{3,2},{4,5},{5,4},{6,7},{7,6},{8,9},{9,8},{10,11... | collective-permute-start | bytes 2359304 | tf_op jit(solution)/shard_map/ppermute | solution.py:351
  167.0 1.1 copy-start.1
  179.5 21.5 %collective-permute-start.7 = (bf16[512,768]{1,0:T(8,128)(2,1)}, bf16[512,768]{1,0:T(8,128)(2,1)S(1)}, u32[]{:S(2)}, u32[]{:S(2)}) collective-permute-start(bf16[512,768]{1,0:T(8,128)(2,1)} %collective-permute-done.6.own_ref), channel_id=1, source_target_pairs={{0,1},{1,0},{2,3},{3,2},{4,5},{5,4},{6,7},{7,6},{8,9},{9,8},{10,11... | collective-permute-start | bytes 2359304 | tf_op jit(solution)/shard_map/ppermute | solution.py:351
  179.6 35.1 %collective-permute-start.5 = (bf16[512,768]{1,0:T(8,128)(2,1)}, bf16[512,768]{1,0:T(8,128)(2,1)S(1)}, u32[]{:S(2)}, u32[]{:S(2)}) collective-permute-start(bf16[512,768]{1,0:T(8,128)(2,1)} %collective-permute-done.4.own_ref), channel_id=1, source_target_pairs={{0,1},{1,0},{2,3},{3,2},{4,5},{5,4},{6,7},{7,6},{8,9},{9,8},{10,11... | collective-permute-start | bytes 2359304 | tf_op jit(solution)/shard_map/ppermute | solution.py:351
  180.0 50.2 %collective-permute-start.3 = (bf16[512,768]{1,0:T(8,128)(2,1)}, bf16[512,768]{1,0:T(8,128)(2,1)S(1)}, u32[]{:S(2)}, u32[]{:S(2)}) collective-permute-start(bf16[512,768]{1,0:T(8,128)(2,1)} %collective-permute-done.2.own_ref), channel_id=1, source_target_pairs={{0,1},{1,0},{2,3},{3,2},{4,5},{5,4},{6,7},{7,6},{8,9},{9,8},{10,11... | collective-permute-start | bytes 2359304 | tf_op jit(solution)/shard_map/ppermute | solution.py:351
  180.2 67.6 %collective-permute-start.1 = (bf16[512,768]{1,0:T(8,128)(2,1)}, bf16[512,768]{1,0:T(8,128)(2,1)S(1)}, u32[]{:S(2)}, u32[]{:S(2)}) collective-permute-start(bf16[512,768]{1,0:T(8,128)(2,1)} %collective-permute-done.own_ref), channel_id=1, source_target_pairs={{0,1},{1,0},{2,3},{3,2},{4,5},{5,4},{6,7},{7,6},{8,9},{9,8},{10,11... | collective-permute-start | bytes 2359304 | tf_op jit(solution)/shard_map/ppermute | solution.py:351
  267.4 3.7 %collective-permute-start.15 = (f32[4,1,512]{2,1,0:T(1,128)S(1)}, f32[4,1,512]{2,1,0:T(1,128)S(1)}, u32[]{:S(2)}, u32[]{:S(2)}) collective-permute-start(f32[4,1,512]{2,1,0:T(1,128)S(1)} %get-tuple-element.72), channel_id=1, source_target_pairs={{0,2},{1,3},{2,0},{3,1},{4,6},{5,7},{6,4},{7,5},{8,10},{9,11},{10,... | collective-permute-start | bytes 24584 | tf_op jit(solution)/shard_map/ppermute | solution.py:348
  271.1 3.7 %collective-permute-start.16 = (f32[2,2,512]{2,1,0:T(2,128)S(1)}, f32[2,2,512]{2,1,0:T(2,128)S(1)}, u32[]{:S(2)}, u32[]{:S(2)}) collective-permute-start(f32[2,2,512]{2,1,0:T(2,128)S(1)} %get-tuple-element.70), channel_id=1, source_target_pairs={{0,4},{1,5},{2,6},{3,7},{4,0},{5,1},{6,2},{7,3},{8,12},{9,13},{10,... | collective-permute-start | bytes 24584 | tf_op jit(solution)/shard_map/ppermute | solution.py:348
  274.9 8.8 %collective-permute-start.17 = (f32[1,4,512]{2,0,1:T(1,128)S(1)}, f32[1,4,512]{2,0,1:T(1,128)S(1)}, u32[]{:S(2)}, u32[]{:S(2)}) collective-permute-start(f32[1,4,512]{2,0,1:T(1,128)S(1)} %get-tuple-element.68), channel_id=1, source_target_pairs={{0,8},{1,9},{2,10},{3,11},{4,12},{5,13},{6,14},{7,15},{8,0},{9,1},... | collective-permute-start | bytes 24584 | tf_op jit(solution)/shard_map/ppermute | solution.py:348
